TPU v7x, 32 devices: a whole 2x2x4 slice. The times are simulated.
32 devices in a mesh: exp: 8 (over z, core), rep: 4 (over y, x).
Axes of the slice: x: 2, y: 2, z: 4, core: 2. Of those that a mesh axis runs over, the one named last changes fastest.
Arguments:
- tokens: bfloat16 [4096, 1536], P(('exp', 'rep')), may hold values from -6 to 6
- grad_out: bfloat16 [4096, 1536], P(('exp', 'rep')), may hold values from -6 to 6
- expert_ids: int32 [4096, 2], P(('exp', 'rep')), may hold values from 0 to 7, all different within a row; in each aligned block of 128 rows (0 to 127, 128 to 255, ...) at most 40 rows name the same one
- probs: bfloat16 [4096, 2], P(('exp', 'rep')), may hold values from 0.099609375 to 1
- w_gate: bfloat16 [8, 768, 1536], P('exp', 'rep'), may hold values from -0.15625 to 0.15625
- w_up: bfloat16 [8, 768, 1536], P('exp', 'rep'), may hold values from -0.15625 to 0.15625
- w_down: bfloat16 [8, 768, 1536], P('exp', 'rep'), may hold values from -0.21875 to 0.21875
Outputs:
- grad_tokens: bfloat16 [4096, 1536], P(('exp', 'rep'))
- grad_probs: float32 [4096, 2], P(('exp', 'rep'))
- grad_gate: float32 [8, 768, 1536], P('exp', 'rep')
- grad_up: float32 [8, 768, 1536], P('exp', 'rep')
- grad_down: float32 [8, 768, 1536], P('exp', 'rep')
Inputs may be any that keep to these rules, and one draw needn't show every extreme that they name: `expert_ids`: each token names two different experts; among the 128 tokens of one device no expert is named more than 40 times, a bound that some block reaches.
All inputs are finite; a program needn't handle non-finite values.
Results may differ from a plain program's by a relative error of at most 0.007.
Values may be sent and summed in bfloat16 or wider, within the bound.
A program may use at most 64 MiB of HBM per device.

v0:
```python
import jax
import jax.numpy as jnp
from jax import lax
from jax.sharding import PartitionSpec as P


def swapped(value, axis, stride):
    return lax.ppermute(value, axis, [(i, i ^ 1 << stride) for i in range(lax.axis_size(axis))])


def pair_gather(parts, along, bit_list, mover):
    for bit in bit_list:
        other = mover(parts, bit)
        upper_bit = lax.axis_index("rep") // (1 << bit) % 2

        def joined_pair(mine, theirs, upper_bit=upper_bit):
            length = mine.shape[along]
            shape_out = mine.shape[:along] + (2 * length,) + mine.shape[along + 1 :]
            joined = jnp.zeros(shape_out, mine.dtype)
            joined = lax.dynamic_update_slice_in_dim(joined, mine, upper_bit * length, along)
            return lax.dynamic_update_slice_in_dim(joined, theirs, (1 - upper_bit) * length, along)

        parts = jax.tree.map(joined_pair, parts, other)
    return parts


def split_halves(parts, along, upper_bit):

    def keep_part(whole):
        length = whole.shape[along] // 2
        return lax.dynamic_slice_in_dim(whole, upper_bit * length, length, along)

    def send_part(whole):
        length = whole.shape[along] // 2
        return lax.dynamic_slice_in_dim(whole, (1 - upper_bit) * length, length, along)

    return (jax.tree.map(keep_part, parts), jax.tree.map(send_part, parts))


def pair_reduce(parts, along, bit_list, mover):
    for bit in reversed(bit_list):
        upper_bit = lax.axis_index("rep") // (1 << bit) % 2
        keep, outgoing = split_halves(parts, along, upper_bit)
        received = mover(outgoing, bit)
        parts = jax.tree.map(jnp.add, keep, received)
    return parts


def half_sum(parts, mover):
    upper_bit = lax.axis_index("rep") % 2
    keep, outgoing = split_halves(parts, 1, upper_bit)
    received = mover(outgoing)
    return jax.tree.map(
        lambda mine, theirs: (mine.astype(jnp.float32) + theirs.astype(jnp.float32)).astype(
            jnp.bfloat16
        ),
        keep,
        received,
    )


def shards(tokens, grad_out, expert_ids, probs, w_gate, w_up, w_down):
    token_count = tokens.shape[0]
    width = tokens.shape[1]
    exp_count = lax.axis_size("exp")
    capacity = 5 * token_count // (2 * exp_count)
    slots = exp_count * capacity
    chosen = expert_ids.reshape(-1)
    onehot = (chosen[:, None] == jnp.arange(exp_count, dtype=jnp.int32)[None, :]).astype(jnp.int32)
    ranks = jnp.sum((jnp.cumsum(onehot, axis=0) - 1) * onehot, axis=1)
    slot_of = chosen * capacity + ranks
    routing = (slot_of[None, :] == jnp.arange(slots, dtype=jnp.int32)[:, None]).astype(jnp.bfloat16)
    token_routing = routing.reshape(slots, token_count, 2).sum(axis=2)
    prob_pairs = probs.reshape(-1, 1)
    send_tokens = (
        jnp.dot(token_routing, tokens, preferred_element_type=jnp.float32)
        .astype(jnp.bfloat16)
        .reshape(exp_count, 1, capacity, width)
    )
    send_grads = (
        jnp.dot(token_routing, grad_out, preferred_element_type=jnp.float32)
        .astype(jnp.bfloat16)
        .reshape(exp_count, 1, capacity, width)
    )
    send_probs = (
        jnp.dot(routing, prob_pairs, preferred_element_type=jnp.float32)
        .astype(jnp.bfloat16)
        .reshape(exp_count, 1, capacity)
    )
    slice_bits = [0]
    replica_bits = list(range(1, lax.axis_size("rep").bit_length() - 1))
    arrived = (
        lax.all_to_all(send_tokens, "exp", split_axis=0, concat_axis=0, tiled=True),
        lax.all_to_all(send_grads, "exp", split_axis=0, concat_axis=0, tiled=True),
        lax.all_to_all(send_probs, "exp", split_axis=0, concat_axis=0, tiled=True),
    )
    arrived = pair_gather(
        arrived,
        1,
        slice_bits,
        lambda parts, bit: swapped((parts[0], parts[1], parts[2]), "rep", bit),
    )
    full_weights = pair_gather(
        (w_gate, w_up, w_down),
        1,
        replica_bits,
        lambda parts, bit: swapped((parts[0], parts[1], parts[2]), "rep", bit),
    )
    gate_w = full_weights[0][0]
    up_w = full_weights[1][0]
    down_w = full_weights[2][0]
    rows = arrived[0].reshape(-1, width)
    grads = arrived[1].reshape(-1, width)
    weight = arrived[2].reshape(-1, 1).astype(jnp.float32)
    gate = jnp.dot(rows, gate_w.T, preferred_element_type=jnp.float32)
    up = jnp.dot(rows, up_w.T, preferred_element_type=jnp.float32)
    sig = jax.nn.sigmoid(gate)
    act = gate * sig
    hidden = act * up
    back = jnp.dot(grads, down_w.T, preferred_element_type=jnp.float32)
    prob_part = jnp.sum(hidden * back, axis=1)
    d_gate = (weight * back * up * sig * (1.0 + gate * (1.0 - sig))).astype(jnp.bfloat16)
    d_up = (weight * back * act).astype(jnp.bfloat16)
    weighted = (weight * hidden).astype(jnp.bfloat16)
    partial_rows = jnp.dot(d_gate, gate_w, preferred_element_type=jnp.float32) + jnp.dot(
        d_up, up_w, preferred_element_type=jnp.float32
    )
    partial_rows = partial_rows.astype(jnp.bfloat16).reshape(exp_count, 2, capacity, width)
    partial_probs = prob_part.astype(jnp.bfloat16).reshape(exp_count, 2, capacity)
    local_gate = jnp.dot(d_gate.T, rows, preferred_element_type=jnp.float32)[None]
    local_up = jnp.dot(d_up.T, rows, preferred_element_type=jnp.float32)[None]
    local_down = jnp.dot(weighted.T, grads, preferred_element_type=jnp.float32)[None]
    summed = half_sum(
        (partial_rows, partial_probs), lambda parts: swapped((parts[0], parts[1]), "rep", 0)
    )
    returned = (
        lax.all_to_all(summed[0], "exp", split_axis=0, concat_axis=0, tiled=True),
        lax.all_to_all(summed[1], "exp", split_axis=0, concat_axis=0, tiled=True),
    )
    weight_grads = pair_reduce(
        (local_gate, local_up, local_down),
        1,
        replica_bits,
        lambda parts, bit: swapped((parts[0], parts[1], parts[2]), "rep", bit),
    )
    slot_rows_back = returned[0].reshape(slots, width)
    slot_probs_back = returned[1].reshape(slots, 1)
    grad_tokens = jnp.dot(
        token_routing.T, slot_rows_back, preferred_element_type=jnp.float32
    ).astype(jnp.bfloat16)
    grad_probs = jnp.dot(routing.T, slot_probs_back, preferred_element_type=jnp.float32).reshape(
        token_count, 2
    )
    return (grad_tokens, grad_probs, weight_grads[0], weight_grads[1], weight_grads[2])


def solution(mesh):
    in_specs = (
        P(("exp", "rep"), None),
        P(("exp", "rep"), None),
        P(("exp", "rep"), None),
        P(("exp", "rep"), None),
        P("exp", "rep", None),
        P("exp", "rep", None),
        P("exp", "rep", None),
    )
    out_specs = (
        P(("exp", "rep"), None),
        P(("exp", "rep"), None),
        P("exp", "rep", None),
        P("exp", "rep", None),
        P("exp", "rep", None),
    )
    return jax.shard_map(shards, mesh=mesh, in_specs=in_specs, out_specs=out_specs, check_vma=False)
```

profile of v0, /device:TPU:0, one launch (start us, length us, event | category | flops | bytes accessed | tf_op | source)
XLA Modules:
  0.0 197.0 jit_solution(4111937065758587337)
XLA Ops:
  4.6 6.3 %all-to-all-start = ((bf16[8,1,40]{2,1,0:T(2,128)(2,1)}), bf16[8,1,40]{2,1,0:T(2,128)(2,1)S(1)}, u32[]{:S(2)}, u32[]{:S(2)}) async-start(bf16[8,1,40]{2,1,0:T(2,128)(2,1)} %reshape.150), calls=%async_computation | async-start | bytes 8192 | tf_op jit(solution)/shard_map/all_to_all | solution.py:95
  11.9 1.3 convolution_convert_fusion
  13.2 3.2 %all-to-all-done = bf16[8,1,40]{2,1,0:T(2,128)(2,1)S(1)} async-done(((bf16[8,1,40]{2,1,0:T(2,128)(2,1)}), bf16[8,1,40]{2,1,0:T(2,128)(2,1)S(1)}, u32[]{:S(2)}, u32[]{:S(2)}) %all-to-all-start) | async-done | bytes 672 | tf_op jit(solution)/shard_map/all_to_all | solution.py:95
  16.4 4.2 %all-to-all-start.2 = ((bf16[8,1,40,1536]{3,2,1,0:T(8,128)(2,1)}), bf16[8,1,40,1536]{3,2,1,0:T(8,128)(2,1)}, u32[]{:S(2)}, u32[]{:S(2)}) async-start(bf16[8,1,40,1536]{3,2,1,0:T(8,128)(2,1)} %bitcast.8), calls=%async_computation.2 | async-start | bytes 1966080 | tf_op jit(solution)/shard_map/all_to_all | solution.py:93
  20.6 1.6 collective-permute-start.5
  22.7 1.5 collective-permute-start.2
  24.5 1.1 bitcast_dynamic-update-slice_fusion.3
  25.6 1.3 convolution_convert_fusion.1
  26.9 18.9 %all-to-all-done.2 = bf16[8,1,40,1536]{3,2,1,0:T(8,128)(2,1)} async-done(((bf16[8,1,40,1536]{3,2,1,0:T(8,128)(2,1)}), bf16[8,1,40,1536]{3,2,1,0:T(8,128)(2,1)}, u32[]{:S(2)}, u32[]{:S(2)}) %all-to-all-start.2) | async-done | bytes 983072 | tf_op jit(solution)/shard_map/all_to_all | solution.py:93
  45.8 4.2 %all-to-all-start.1 = ((bf16[8,1,40,1536]{3,2,1,0:T(8,128)(2,1)}), bf16[8,1,40,1536]{3,2,1,0:T(8,128)(2,1)}, u32[]{:S(2)}, u32[]{:S(2)}) async-start(bf16[8,1,40,1536]{3,2,1,0:T(8,128)(2,1)} %bitcast.73), calls=%async_computation.1 | async-start | bytes 1966080 | tf_op jit(solution)/shard_map/all_to_all | solution.py:94
  51.1 1.9 bitcast_dynamic-update-slice_fusion.5
  53.1 1.5 collective-permute-start
  54.6 2.1 %collective-permute-done = bf16[8,1,40]{2,1,0:T(2,128)(2,1)S(1)} collective-permute-done((bf16[8,1,40]{2,1,0:T(2,128)(2,1)S(1)}, bf16[8,1,40]{2,1,0:T(2,128)(2,1)S(1)}, u32[]{:S(2)}, u32[]{:S(2)}) %collective-permute-start) | collective-permute-done | bytes 672 | tf_op jit(solution)/shard_map/ppermute | solution.py:8
  56.8 1.1 bitcast_dynamic-update-slice_fusion
  57.9 1.1 bitcast_dynamic-update-slice_fusion.2
  59.1 1.6 collective-permute-start.3
  61.6 1.9 bitcast_dynamic-update-slice_fusion.4
  63.5 11.7 %all-to-all-done.1 = bf16[8,1,40,1536]{3,2,1,0:T(8,128)(2,1)} async-done(((bf16[8,1,40,1536]{3,2,1,0:T(8,128)(2,1)}), bf16[8,1,40,1536]{3,2,1,0:T(8,128)(2,1)}, u32[]{:S(2)}, u32[]{:S(2)}) %all-to-all-start.1) | async-done | bytes 983072 | tf_op jit(solution)/shard_map/all_to_all | solution.py:94
  75.2 1.5 collective-permute-start.1
  76.9 1.3 constant_dynamic-update-slice_fusion.1
  78.4 1.3 constant_dynamic-update-slice_fusion.3
  79.7 4.4 %collective-permute-done.3 = bf16[8,1,40,1536]{3,2,1,0:T(8,128)(2,1)} collective-permute-done((bf16[8,1,40,1536]{3,2,1,0:T(8,128)(2,1)}, bf16[8,1,40,1536]{3,2,1,0:T(8,128)(2,1)}, u32[]{:S(2)}, u32[]{:S(2)}) %collective-permute-start.3) | collective-permute-done | bytes 983072 | tf_op jit(solution)/shard_map/ppermute | solution.py:8
  84.1 1.3 constant_dynamic-update-slice_fusion
  85.4 1.1 fusion.16
  86.5 1.1 fusion.15
  87.7 16.0 %collective-permute-done.1 = bf16[8,1,40,1536]{3,2,1,0:T(8,128)(2,1)S(1)} collective-permute-done((bf16[8,1,40,1536]{3,2,1,0:T(8,128)(2,1)}, bf16[8,1,40,1536]{3,2,1,0:T(8,128)(2,1)S(1)}, u32[]{:S(2)}, u32[]{:S(2)}) %collective-permute-start.1) | collective-permute-done | bytes 983072 | tf_op jit(solution)/shard_map/ppermute | solution.py:8
  103.8 1.1 fusion.1
  104.9 4.3 %multiply_reduce_fusion = (bf16[640]{0:T(1024)(128)(2,1)S(1)}, bf16[640,384]{0,1:T(8,128)(2,1)}, bf16[640,384]{0,1:T(8,128)(2,1)S(1)}) fusion(f32[640,384]{0,1:T(8,128)S(1)} %fusion.15, f32[640,384]{0,1:T(8,128)S(1)} %fusion.16, f32[640]{0:T(1024)S(1)} %reshape.144, bf16[640,1536]{1,0:T(8,128)(2,1)S(1)} %bitcast.76, ...), kind=kOutput, calls=%fused_computation.13 | convolution fusion | flops 759152000 | bytes 6098688 | tf_op jit(solution)/shard_map/dot_general | solution.py:120
  109.2 2.5 %fusion.19 = f32[384,1536]{1,0:T(8,128)} fusion(bf16[640,384]{0,1:T(8,128)(2,1)S(1)} %get-tuple-element.7, bf16[640,1536]{1,0:T(8,128)(2,1)S(1)} %bitcast.79), kind=kOutput, calls=%fused_computation.57 | convolution fusion | flops 754974720 | bytes 4816896 | tf_op jit(solution)/shard_map/dot_general | solution.py:131
  111.7 3.2 %fusion.17 = f32[640,1536]{1,0:T(8,128)} fusion(bf16[640,384]{0,1:T(8,128)(2,1)S(1)} %get-tuple-element.7, bf16[384,1536]{1,0:T(8,128)(2,1)S(1)} %bitcast_dynamic-update-slice_fusion.2), kind=kOutput, calls=%fused_computation.55 | convolution fusion | flops 754974720 | bytes 5603328 | tf_op jit(solution)/shard_map/dot_general | solution.py:125
  114.9 1.1 dynamic-slice_bitcast_fusion
  116.0 1.5 collective-permute-start.10
  117.6 1.6 collective-permute-start.7
  119.2 3.5 %add_convert_fusion = bf16[640,1536]{1,0:T(8,128)(2,1)S(1)} fusion(f32[640,1536]{1,0:T(8,128)} %fusion.17, bf16[640,384]{0,1:T(8,128)(2,1)} %get-tuple-element.6, bf16[384,1536]{1,0:T(8,128)(2,1)S(1)} %bitcast_dynamic-update-slice_fusion), kind=kOutput, calls=%fused_computation | convolution fusion | flops 756940800 | bytes 7569408 | tf_op jit(solution)/shard_map/dot_general | solution.py:125
  124.6 2.5 %fusion.18 = f32[384,1536]{1,0:T(8,128)} fusion(bf16[640,384]{0,1:T(8,128)(2,1)S(1)} %copy-done.10, bf16[640,1536]{1,0:T(8,128)(2,1)S(1)} %bitcast.80), kind=kOutput, calls=%fused_computation.56 | convolution fusion | flops 754974720 | bytes 4816896 | tf_op jit(solution)/shard_map/dot_general | solution.py:130
  129.3 4.8 %all-to-all-start.4 = ((bf16[8,1,40]{2,1,0:T(2,128)(2,1)}), bf16[8,1,40]{2,1,0:T(2,128)(2,1)S(1)}, u32[]{:S(2)}, u32[]{:S(2)}) async-start(bf16[8,1,40]{2,1,0:T(2,128)(2,1)} %copy.69), calls=%async_computation.4 | async-start | bytes 8192 | tf_op jit(solution)/shard_map/all_to_all | solution.py:138
  134.1 2.4 %dynamic-slice_bitcast_fusion.2 = f32[1,192,1536]{2,1,0:T(8,128)} fusion(f32[384,1536]{1,0:T(8,128)} %fusion.18, s32[]{:T(128)S(6)} %select_n.57), kind=kLoop, calls=%fused_computation.10 | loop fusion | bytes 2359300 | tf_op jit(solution)/shard_map/dynamic_slice | solution.py:35
  136.4 1.5 collective-permute-start.8
  138.0 1.7 all-to-all-done.4
  139.8 6.0 %collective-permute-done.6 = bf16[8,1,40,1536]{3,2,1,0:T(8,128)(2,1)S(1)} collective-permute-done((bf16[8,1,40,1536]{3,2,1,0:T(8,128)(2,1)}, bf16[8,1,40,1536]{3,2,1,0:T(8,128)(2,1)S(1)}, u32[]{:S(2)}, u32[]{:S(2)}) %collective-permute-start.6) | collective-permute-done | bytes 983072 | tf_op jit(solution)/shard_map/ppermute | solution.py:8
  145.8 1.2 add_convert_fusion.1
  147.0 4.5 %all-to-all-start.3 = ((bf16[8,1,40,1536]{3,2,1,0:T(8,128)(2,1)}), bf16[8,1,40,1536]{3,2,1,0:T(8,128)(2,1)S(1)}, u32[]{:S(2)}, u32[]{:S(2)}) async-start(bf16[8,1,40,1536]{3,2,1,0:T(8,128)(2,1)} %add_convert_fusion.1), calls=%async_computation.3 | async-start | bytes 1966080 | tf_op jit(solution)/shard_map/all_to_all | solution.py:137
  152.2 2.8 %bitcast_add_fusion = f32[1,192,1536]{2,1,0:T(8,128)} fusion(f32[1,192,1536]{2,1,0:T(8,128)} %collective-permute-done.10, f32[384,1536]{1,0:T(8,128)} %copy-done.1, s32[]{:T(128)S(6)} %select_n.56), kind=kLoop, calls=%fused_computation.5 | loop fusion | flops 294912 | bytes 3538948 | tf_op jit(solution)/shard_map/add | solution.py:45
  155.0 15.5 %collective-permute-done.9 = f32[1,192,1536]{2,1,0:T(8,128)} collective-permute-done((f32[1,192,1536]{2,1,0:T(8,128)}, f32[1,192,1536]{2,1,0:T(8,128)}, u32[]{:S(2)}, u32[]{:S(2)}) %collective-permute-start.9) | collective-permute-done | bytes 1179680 | tf_op jit(solution)/shard_map/ppermute | solution.py:8
  170.5 2.5 %bitcast_add_fusion.1 = f32[1,192,1536]{2,1,0:T(8,128)} fusion(f32[1,192,1536]{2,1,0:T(8,128)} %collective-permute-done.9, f32[384,1536]{1,0:T(8,128)S(1)} %copy-done.3, s32[]{:T(128)S(6)} %select_n.56), kind=kLoop, calls=%fused_computation.6 | loop fusion | flops 294912 | bytes 3538948 | tf_op jit(solution)/shard_map/add | solution.py:45
  172.9 20.5 %collective-permute-done.8 = f32[1,192,1536]{2,1,0:T(8,128)} collective-permute-done((f32[1,192,1536]{2,1,0:T(8,128)}, f32[1,192,1536]{2,1,0:T(8,128)}, u32[]{:S(2)}, u32[]{:S(2)}) %collective-permute-start.8) | collective-permute-done | bytes 1179680 | tf_op jit(solution)/shard_map/ppermute | solution.py:8
  193.4 2.5 %bitcast_add_fusion.2 = f32[1,192,1536]{2,1,0:T(8,128)} fusion(f32[1,192,1536]{2,1,0:T(8,128)} %collective-permute-done.8, f32[384,1536]{1,0:T(8,128)S(1)} %copy-done.4, s32[]{:T(128)S(6)} %select_n.56), kind=kLoop, calls=%fused_computation.7 | loop fusion | flops 294912 | bytes 3538948 | tf_op jit(solution)/shard_map/add | solution.py:45
  195.9 1.2 convolution_convert_fusion.2
  (72 shorter events, 13.3 us)
Async XLA Ops:
  0.6 11.2 %copy-start = (bf16[128,1536]{1,0:T(8,128)(2,1)S(1)}, bf16[128,1536]{1,0:T(8,128)(2,1)}, u32[]{:S(2)}) copy-start(bf16[128,1536]{1,0:T(8,128)(2,1)} %param.7) | copy-start | bytes 1179652
  1.6 19.0 %copy-start.9 = (bf16[1,192,1536]{2,1,0:T(8,128)(2,1)S(1)}, bf16[1,192,1536]{2,1,0:T(8,128)(2,1)}, u32[]{:S(2)}) copy-start(bf16[1,192,1536]{2,1,0:T(8,128)(2,1)} %param.11) | copy-start | bytes 1769476
  4.6 11.8 %all-to-all-start = ((bf16[8,1,40]{2,1,0:T(2,128)(2,1)}), bf16[8,1,40]{2,1,0:T(2,128)(2,1)S(1)}, u32[]{:S(2)}, u32[]{:S(2)}) async-start(bf16[8,1,40]{2,1,0:T(2,128)(2,1)} %reshape.150), calls=%async_computation | async-start | bytes 8192 | tf_op jit(solution)/shard_map/all_to_all | solution.py:95
  11.9 13.7 %copy-start.7 = (bf16[320,128]{1,0:T(8,128)(2,1)}, bf16[320,128]{1,0:T(8,128)(2,1)S(1)}, u32[]{:S(2)}) copy-start(bf16[320,128]{1,0:T(8,128)(2,1)S(1)} %fusion.9) | copy-start | bytes 245764
  16.4 29.4 %all-to-all-start.2 = ((bf16[8,1,40,1536]{3,2,1,0:T(8,128)(2,1)}), bf16[8,1,40,1536]{3,2,1,0:T(8,128)(2,1)}, u32[]{:S(2)}, u32[]{:S(2)}) async-start(bf16[8,1,40,1536]{3,2,1,0:T(8,128)(2,1)} %bitcast.8), calls=%async_computation.2 | async-start | bytes 1966080 | tf_op jit(solution)/shard_map/all_to_all | solution.py:93
  20.6 36.2 %collective-permute-start.5 = (bf16[1,192,1536]{2,1,0:T(8,128)(2,1)S(1)}, bf16[1,192,1536]{2,1,0:T(8,128)(2,1)}, u32[]{:S(2)}, u32[]{:S(2)}) collective-permute-start(bf16[1,192,1536]{2,1,0:T(8,128)(2,1)S(1)} %copy-done.9), channel_id=1, source_target_pairs={{0,2},{1,3},{2,0},{3,1},{4,6},{5,7},{6,4},{7,5},{8,10},{9,11},{10,... | collective-permute-start | bytes 1769480 | tf_op jit(solution)/shard_map/ppermute | solution.py:8
  22.2 35.7 %collective-permute-start.4 = (bf16[1,192,1536]{2,1,0:T(8,128)(2,1)}, bf16[1,192,1536]{2,1,0:T(8,128)(2,1)}, u32[]{:S(2)}, u32[]{:S(2)}) collective-permute-start(bf16[1,192,1536]{2,1,0:T(8,128)(2,1)} %param.12), channel_id=1, source_target_pairs={{0,2},{1,3},{2,0},{3,1},{4,6},{5,7},{6,4},{7,5},{8,10},{9,11},{10,... | collective-permute-start | bytes 1769480 | tf_op jit(solution)/shard_map/ppermute | solution.py:8
  22.7 38.9 %collective-permute-start.2 = (bf16[1,192,1536]{2,1,0:T(8,128)(2,1)}, bf16[1,192,1536]{2,1,0:T(8,128)(2,1)}, u32[]{:S(2)}, u32[]{:S(2)}) collective-permute-start(bf16[1,192,1536]{2,1,0:T(8,128)(2,1)} %param.13), channel_id=1, source_target_pairs={{0,2},{1,3},{2,0},{3,1},{4,6},{5,7},{6,4},{7,5},{8,10},{9,11},{10,... | collective-permute-start | bytes 1769480 | tf_op jit(solution)/shard_map/ppermute | solution.py:8
  24.3 1.3 copy-start.11
  45.8 29.4 %all-to-all-start.1 = ((bf16[8,1,40,1536]{3,2,1,0:T(8,128)(2,1)}), bf16[8,1,40,1536]{3,2,1,0:T(8,128)(2,1)}, u32[]{:S(2)}, u32[]{:S(2)}) async-start(bf16[8,1,40,1536]{3,2,1,0:T(8,128)(2,1)} %bitcast.73), calls=%async_computation.1 | async-start | bytes 1966080 | tf_op jit(solution)/shard_map/all_to_all | solution.py:94
  53.1 3.6 %collective-permute-start = (bf16[8,1,40]{2,1,0:T(2,128)(2,1)S(1)}, bf16[8,1,40]{2,1,0:T(2,128)(2,1)S(1)}, u32[]{:S(2)}, u32[]{:S(2)}) collective-permute-start(bf16[8,1,40]{2,1,0:T(2,128)(2,1)S(1)} %all-to-all-done), channel_id=1, source_target_pairs={{0,1},{1,0},{2,3},{3,2},{4,5},{5,4},{6,7},{7,6},{8,9},{9,8},{10,11... | collective-permute-start | bytes 1928 | tf_op jit(solution)/shard_map/ppermute | solution.py:8
  59.1 25.1 %collective-permute-start.3 = (bf16[8,1,40,1536]{3,2,1,0:T(8,128)(2,1)}, bf16[8,1,40,1536]{3,2,1,0:T(8,128)(2,1)}, u32[]{:S(2)}, u32[]{:S(2)}) collective-permute-start(bf16[8,1,40,1536]{3,2,1,0:T(8,128)(2,1)} %all-to-all-done.2), channel_id=1, source_target_pairs={{0,1},{1,0},{2,3},{3,2},{4,5},{5,4},{6,7},{7,6},{8,9},{9,8},{10,11... | collective-permute-start | bytes 2949128 | tf_op jit(solution)/shard_map/ppermute | solution.py:8
  75.2 28.4 %collective-permute-start.1 = (bf16[8,1,40,1536]{3,2,1,0:T(8,128)(2,1)}, bf16[8,1,40,1536]{3,2,1,0:T(8,128)(2,1)S(1)}, u32[]{:S(2)}, u32[]{:S(2)}) collective-permute-start(bf16[8,1,40,1536]{3,2,1,0:T(8,128)(2,1)} %all-to-all-done.1), channel_id=1, source_target_pairs={{0,1},{1,0},{2,3},{3,2},{4,5},{5,4},{6,7},{7,6},{8,9},{9,8},{10,11... | collective-permute-start | bytes 2949128 | tf_op jit(solution)/shard_map/ppermute | solution.py:8
  85.4 23.8 %copy-start.5 = (bf16[8,2,40,1536]{3,2,1,0:T(8,128)(2,1)}, bf16[8,2,40,1536]{3,2,1,0:T(8,128)(2,1)S(1)}, u32[]{:S(2)}) copy-start(bf16[8,2,40,1536]{3,2,1,0:T(8,128)(2,1)S(1)} %constant_dynamic-update-slice_fusion) | copy-start | bytes 5898244
  104.9 10.0 %copy-start.1 = (f32[384,1536]{1,0:T(8,128)}, f32[384,1536]{1,0:T(8,128)S(1)}, u32[]{:S(2)}) copy-start(f32[384,1536]{1,0:T(8,128)S(1)} %fusion.1) | copy-start | bytes 7077892
  116.0 36.3 %collective-permute-start.10 = (f32[1,192,1536]{2,1,0:T(8,128)}, f32[1,192,1536]{2,1,0:T(8,128)}, u32[]{:S(2)}, u32[]{:S(2)}) collective-permute-start(f32[1,192,1536]{2,1,0:T(8,128)} %dynamic-slice_bitcast_fusion), channel_id=1, source_target_pairs={{0,2},{1,3},{2,0},{3,1},{4,6},{5,7},{6,4},{7,5},{8,10},{9,11},{10,... | collective-permute-start | bytes 3538952 | tf_op jit(solution)/shard_map/ppermute | solution.py:8
  117.6 11.1 %collective-permute-start.7 = (bf16[8,1,40]{2,0,1:T(8,128)(2,1)S(1)}, bf16[8,1,40]{2,0,1:T(8,128)(2,1)S(1)}, u32[]{:S(2)}, u32[]{:S(2)}) collective-permute-start(bf16[8,1,40]{2,0,1:T(8,128)(2,1)S(1)} %copy.72), channel_id=1, source_target_pairs={{0,1},{1,0},{2,3},{3,2},{4,5},{5,4},{6,7},{7,6},{8,9},{9,8},{10,11... | collective-permute-start | bytes 1928 | tf_op jit(solution)/shard_map/ppermute | solution.py:8
  119.2 5.1 %copy-start.10 = (bf16[640,384]{0,1:T(8,128)(2,1)S(1)}, bf16[640,384]{0,1:T(8,128)(2,1)}, u32[]{:S(2)}) copy-start(bf16[640,384]{0,1:T(8,128)(2,1)} %get-tuple-element.6) | copy-start | bytes 1474564
  122.7 1.9 copy-start.6
  123.7 3.4 %copy-start.2 = (f32[384,1536]{1,0:T(8,128)S(1)}, f32[384,1536]{1,0:T(8,128)}, u32[]{:S(2)}) copy-start(f32[384,1536]{1,0:T(8,128)} %fusion.19) | copy-start | bytes 7077892
  123.7 22.0 %collective-permute-start.6 = (bf16[8,1,40,1536]{3,2,1,0:T(8,128)(2,1)}, bf16[8,1,40,1536]{3,2,1,0:T(8,128)(2,1)S(1)}, u32[]{:S(2)}, u32[]{:S(2)}) collective-permute-start(bf16[8,1,40,1536]{3,2,1,0:T(8,128)(2,1)} %constant_dynamic-slice_fusion.2), channel_id=1, source_target_pairs={{0,1},{1,0},{2,3},{3,2},{4,5},{5,4},{6,7},{7,6},{8,9},{9,8},{10,11... | collective-permute-start | bytes 2949128 | tf_op jit(solution)/shard_map/ppermute | solution.py:8
  128.2 42.3 %collective-permute-start.9 = (f32[1,192,1536]{2,1,0:T(8,128)}, f32[1,192,1536]{2,1,0:T(8,128)}, u32[]{:S(2)}, u32[]{:S(2)}) collective-permute-start(f32[1,192,1536]{2,1,0:T(8,128)} %dynamic-slice_bitcast_fusion.1), channel_id=1, source_target_pairs={{0,2},{1,3},{2,0},{3,1},{4,6},{5,7},{6,4},{7,5},{8,10},{9,11},{10,... | collective-permute-start | bytes 3538952 | tf_op jit(solution)/shard_map/ppermute | solution.py:8
  129.3 10.3 %all-to-all-start.4 = ((bf16[8,1,40]{2,1,0:T(2,128)(2,1)}), bf16[8,1,40]{2,1,0:T(2,128)(2,1)S(1)}, u32[]{:S(2)}, u32[]{:S(2)}) async-start(bf16[8,1,40]{2,1,0:T(2,128)(2,1)} %copy.69), calls=%async_computation.4 | async-start | bytes 8192 | tf_op jit(solution)/shard_map/all_to_all | solution.py:138
  136.4 57.0 %collective-permute-start.8 = (f32[1,192,1536]{2,1,0:T(8,128)}, f32[1,192,1536]{2,1,0:T(8,128)}, u32[]{:S(2)}, u32[]{:S(2)}) collective-permute-start(f32[1,192,1536]{2,1,0:T(8,128)} %dynamic-slice_bitcast_fusion.2), channel_id=1, source_target_pairs={{0,2},{1,3},{2,0},{3,1},{4,6},{5,7},{6,4},{7,5},{8,10},{9,11},{10,... | collective-permute-start | bytes 3538952 | tf_op jit(solution)/shard_map/ppermute | solution.py:8
  147.0 48.9 %all-to-all-start.3 = ((bf16[8,1,40,1536]{3,2,1,0:T(8,128)(2,1)}), bf16[8,1,40,1536]{3,2,1,0:T(8,128)(2,1)S(1)}, u32[]{:S(2)}, u32[]{:S(2)}) async-start(bf16[8,1,40,1536]{3,2,1,0:T(8,128)(2,1)} %add_convert_fusion.1), calls=%async_computation.3 | async-start | bytes 1966080 | tf_op jit(solution)/shard_map/all_to_all | solution.py:137
  151.5 19.0 %copy-start.3 = (f32[384,1536]{1,0:T(8,128)S(1)}, f32[384,1536]{1,0:T(8,128)}, u32[]{:S(2)}) copy-start(f32[384,1536]{1,0:T(8,128)} %fusion.19) | copy-start | bytes 7077892
  155.0 38.4 %copy-start.4 = (f32[384,1536]{1,0:T(8,128)S(1)}, f32[384,1536]{1,0:T(8,128)}, u32[]{:S(2)}) copy-start(f32[384,1536]{1,0:T(8,128)} %fusion.18) | copy-start | bytes 7077892
  172.9 23.0 %copy-start.8 = (bf16[320,128]{1,0:T(8,128)(2,1)S(1)}, bf16[320,128]{1,0:T(8,128)(2,1)}, u32[]{:S(2)}) copy-start(bf16[320,128]{1,0:T(8,128)(2,1)} %copy-done.7) | copy-start | bytes 245764
where the time goes:
time: 198 us; the launch traced here: 197 us
  waiting for transfers between devices  101 us (51%)
  starting transfers between devices  37.9 us (19%)
  matrix products  24.1 us (12%)
  local copies, waits for them, and re-layouts  22.8 us (12%)
  other arithmetic  10.4 us (5%)
    ppermute x11, waiting for transfers between devices, swapped(): lax.ppermute(value, axis, [(i, i ^ 1 << stride) for i in range(lax.axis_s...  65.5 us
    all_to_all x1, waiting for transfers between devices, shards(): lax.all_to_all(send_tokens, 'exp', split_axis=0, concat_axis=0, tiled=True)  18.9 us
    ppermute x11, starting transfers between devices, swapped(): lax.ppermute(value, axis, [(i, i ^ 1 << stride) for i in range(lax.axis_s...  13.8 us
    all_to_all x1, waiting for transfers between devices, shards(): lax.all_to_all(send_grads, 'exp', split_axis=0, concat_axis=0, tiled=True)  11.7 us
    add x3, other arithmetic, pair_reduce(): parts = jax.tree.map(jnp.add, keep, received)  7.69 us
    all_to_all x1, starting transfers between devices, shards(): lax.all_to_all(send_probs, 'exp', split_axis=0, concat_axis=0, tiled=True)  6.33 us
    dynamic_update_slice x6, local copies, waits for them, and re-layouts, joined_pair(): lax.dynamic_update_slice_in_dim(joined, mine, upper_bit * length, along)  5.7 us
    dynamic_slice x4, local copies, waits for them, and re-layouts, send_part(): lax.dynamic_slice_in_dim(whole, (1 - upper_bit) * length, length, along)  5.58 us
  transfers between devices with their start and end apart: 16, of which 11 were waited for; matrix products, arithmetic and copies ran while one was open for 20% of the time, Pallas kernels for 0%

commit v1 on v0

v1 whole, which is shorter than its diff:
```python
import functools

import jax
import jax.numpy as jnp
from jax import lax
from jax.experimental import pallas as pl
from jax.experimental.pallas import tpu as pltpu
from jax.sharding import PartitionSpec as P

F32 = jnp.float32
BF16 = jnp.bfloat16
NT = (((1,), (1,)), ((), ()))
TN = (((0,), (0,)), ((), ()))


def flipped(index, mask, bits):
    for bit in range(bits):
        if mask >> bit & 1:
            index = index + (1 << bit) - 2 * (1 << bit) * (index // (1 << bit) % 2)
    return index


def dot(a, b, dims=(((1,), (0,)), ((), ()))):
    return lax.dot_general(a, b, dims, preferred_element_type=F32)


def layer(
    exp_count,
    rep_count,
    cap,
    select,
    tokens,
    grads,
    w_gate,
    w_up,
    w_down,
    ret,
    ret_prob,
    own_grads,
    peer_grads,
    send,
    recv,
    weights,
    rows,
    row_grads,
    d_gate,
    d_up,
    hid,
    x_send,
    x_recv,
    keep,
    z_send,
    xp_send,
    xp_recv,
    keep_prob,
    zp_send,
    grads_out,
    z_sems,
    x_sems,
    y_sems,
    xr_sems,
    zr_sems,
    xp_sems,
    zp_sems,
    g_sems,
):
    exp_bits = exp_count.bit_length() - 1
    rep_bits = rep_count.bit_length() - 1
    copies = rep_count // 2
    exp_at = lax.axis_index("exp")
    rep_at = lax.axis_index("rep")
    width = tokens.shape[1]
    half = width // 2
    part = w_gate.shape[0]
    hidden = copies * part
    exp_peer = [{"exp": flipped(exp_at, d, exp_bits)} for d in range(exp_count)]
    x_peer = {"rep": flipped(rep_at, 1, rep_bits)}
    y_peer = [{"rep": flipped(rep_at, 2 * f, rep_bits)} for f in range(copies)]

    barrier = pltpu.get_barrier_semaphore()
    peers = exp_peer[1:] + [x_peer] + y_peer[1:]
    for peer in peers:
        pl.semaphore_signal(barrier, inc=1, device_id=peer, device_id_type=pl.DeviceIdType.MESH)
    order = [d for d in range(exp_count // 2, exp_count)] + [d for d in range(exp_count // 2)]
    for d in order:
        picked = dot(select[d, :, : tokens.shape[0]], tokens[...]) + dot(
            select[d, :, tokens.shape[0] :], grads[...]
        )
        send[d] = picked.astype(BF16)
    pl.semaphore_wait(barrier, len(peers))

    started = []

    def remote(src, dst, sems, at, peer):
        copy = pltpu.make_async_remote_copy(
            src_ref=src,
            dst_ref=dst,
            send_sem=sems.at[(0, *at)],
            recv_sem=sems.at[(1, *at)],
            device_id=peer,
            device_id_type=pl.DeviceIdType.MESH,
        )
        copy.start()
        started.append(copy)
        return copy

    z_in, y_in, x_in = {}, {}, {}
    matrices = (w_gate, w_up, w_down)
    for f in range(1, copies):
        for m in range(3):
            y_in[m, f] = remote(matrices[m], weights.at[m, f], y_sems, (m, f), y_peer[f])
    for d in order:
        if d:
            z_in[d] = remote(send.at[d], recv.at[0, d], z_sems, (d,), exp_peer[d])
    x_in[0] = remote(send.at[0], recv.at[1, 0], x_sems, (0,), x_peer)
    recv[0, 0] = send[0]
    for m in range(3):
        weights[m, 0] = matrices[m][...]
    for d in range(1, exp_count):
        z_in[d].wait_recv()
        x_in[d] = remote(recv.at[0, d], recv.at[1, d], x_sems, (d,), x_peer)
        if d == exp_count // 2 - 1:
            for copy in y_in.values():
                copy.wait_recv()

    ones = jnp.ones((16, hidden), BF16)
    pad = jnp.zeros((128 - cap, hidden), F32)
    xr_in, xp_in = {}, {}
    matrix = [weights.at[m] for m in range(3)]

    def whole(m):
        return matrix[m][...].reshape(hidden, width)

    def forward(step):
        pieces_t, pieces_g = [], []
        for d in (2 * step, 2 * step + 1):
            x_in[d].wait_recv()
            for side in (0, 1):
                block = recv[side, d].astype(F32)
                pieces_t.append(block[:cap])
                pieces_g.append(block[cap:])
        at = pl.ds(step * 4 * cap, 4 * cap)
        rows_s = jnp.concatenate(pieces_t, axis=0).astype(BF16)
        grads_s = jnp.concatenate(pieces_g, axis=0).astype(BF16)
        rows[at] = rows_s
        row_grads[at] = grads_s
        gate = dot(rows_s, whole(0), NT)
        up = dot(rows_s, whole(1), NT)
        back = dot(grads_s, whole(2), NT)
        sig = jax.nn.sigmoid(gate)
        act = gate * sig
        hid_s = act * up
        d_gate[at] = (back * up * sig * (1.0 + gate * (1.0 - sig))).astype(BF16)
        d_up[at] = (back * act).astype(BF16)
        hid[at] = hid_s.astype(BF16)
        product = hid_s * back
        for i in range(4):
            d, side = 2 * step + i // 2, i % 2
            mine = jnp.concatenate([product[i * cap : (i + 1) * cap], pad], axis=0).astype(BF16)
            total = dot(ones, mine, NT)
            if side:
                xp_send[d] = total.astype(BF16)
                xp_in[d] = remote(xp_send.at[d], xp_recv.at[d], xp_sems, (d,), x_peer)
            else:
                keep_prob[d] = total

    def backward(step):
        at = pl.ds(step * 4 * cap, 4 * cap)
        partial = dot(d_gate[at], whole(0)) + dot(d_up[at], whole(1))
        for i in range(4):
            d, side = 2 * step + i // 2, i % 2
            piece = partial[i * cap : (i + 1) * cap]
            folded = jnp.concatenate([piece[:, :half], piece[:, half:]], axis=0)
            if side:
                x_send[d] = folded.astype(BF16)
                xr_in[d] = remote(x_send.at[d], x_recv.at[d], xr_sems, (d,), x_peer)
            else:
                keep[d] = folded

    zr_in = []

    def give_back(d):
        xp_in[d].wait_recv()
        xr_in[d].wait_recv()
        total = (keep[d] + x_recv[d].astype(F32)).astype(BF16)
        total_prob = (keep_prob[d] + xp_recv[d].astype(F32)).astype(BF16)
        if d == 0:
            ret[0] = total
            ret_prob[0] = total_prob
        else:
            z_send[d] = total
            zp_send[d] = total_prob
            zr_in.append(remote(z_send.at[d], ret.at[d], zr_sems, (d,), exp_peer[d]))
            zr_in.append(remote(zp_send.at[d], ret_prob.at[d], zp_sems, (d,), exp_peer[d]))

    steps = exp_count // 2
    for step in range(steps):
        forward(step)
        if step < steps - 1:
            backward(step)

    g_in = []
    lefts = (d_gate, d_up, hid)
    rights = (rows, rows, row_grads)
    for m in range(3):
        for f in range(1, copies):
            product = dot(lefts[m][:, f * part : (f + 1) * part], rights[m][...], TN)
            grads_out[m, f] = product.astype(BF16)
            g_in.append(remote(grads_out.at[m, f], peer_grads.at[m, f - 1], g_sems, (m, f), y_peer[f]))
        if m == 0:
            backward(steps - 1)
            for d in range(exp_count // 2):
                give_back(d)
    for m in range(3):
        own_grads[m] = dot(lefts[m][:, :part], rights[m][...], TN)
        if m == 1:
            for d in range(exp_count // 2, exp_count):
                give_back(d)
    for copy in zr_in + g_in:
        copy.wait_recv()
    for copy in started:
        copy.wait_send()


def shards(rep_count, tokens, grad_out, expert_ids, probs, w_gate, w_up, w_down):
    count, width = tokens.shape
    exp_count = lax.axis_size("exp")
    copies = rep_count // 2
    part = w_gate.shape[1]
    hidden = copies * part
    cap = -(-(5 * count // (2 * exp_count)) // 8) * 8
    slots = exp_count * cap
    half = width // 2
    chosen = expert_ids.reshape(-1)
    pair = jnp.arange(2 * count, dtype=jnp.int32)
    same = (chosen[:, None] == chosen[None, :]) & (pair[None, :] < pair[:, None])
    ranks = jnp.sum(same.astype(jnp.int32), axis=1)
    slot_of = (chosen ^ lax.axis_index("exp")) * cap + ranks
    slot_pair = slot_of.reshape(count, 2)
    slot = jnp.arange(slots, dtype=jnp.int32)[:, None]
    hits = [slot_pair[:, k][None, :] == slot for k in (0, 1)]
    picks = (hits[0] | hits[1]).astype(BF16)
    scaled = jnp.where(hits[0], probs[:, 0][None, :], jnp.where(hits[1], probs[:, 1][None, :], 0))
    zero = jnp.zeros((exp_count, cap, count), BF16)
    select = jnp.concatenate(
        [
            jnp.concatenate([picks.reshape(exp_count, cap, count), zero], axis=2),
            jnp.concatenate([zero, scaled.astype(BF16).reshape(exp_count, cap, count)], axis=2),
        ],
        axis=1,
    )
    vmem = pl.BlockSpec(memory_space=pltpu.VMEM)
    total_rows = 2 * slots
    blocks = (exp_count, 2 * cap, half)
    dma = pltpu.SemaphoreType.DMA
    ret, ret_prob, own_grads, peer_grads = pl.pallas_call(
        functools.partial(layer, exp_count, rep_count, cap),
        out_shape=(
            jax.ShapeDtypeStruct(blocks, BF16),
            jax.ShapeDtypeStruct((exp_count, 16, 128), BF16),
            jax.ShapeDtypeStruct((3, part, width), F32),
            jax.ShapeDtypeStruct((3, copies - 1, part, width), BF16),
        ),
        in_specs=[vmem] * 6,
        out_specs=(vmem,) * 4,
        scratch_shapes=[
            pltpu.VMEM((exp_count, 2 * cap, width), BF16),
            pltpu.VMEM((2, exp_count, 2 * cap, width), BF16),
            pltpu.VMEM((3, copies, part, width), BF16),
            pltpu.VMEM((total_rows, width), BF16),
            pltpu.VMEM((total_rows, width), BF16),
            pltpu.VMEM((total_rows, hidden), BF16),
            pltpu.VMEM((total_rows, hidden), BF16),
            pltpu.VMEM((total_rows, hidden), BF16),
            pltpu.VMEM(blocks, BF16),
            pltpu.VMEM(blocks, BF16),
            pltpu.VMEM(blocks, F32),
            pltpu.VMEM(blocks, BF16),
            pltpu.VMEM((exp_count, 16, 128), BF16),
            pltpu.VMEM((exp_count, 16, 128), BF16),
            pltpu.VMEM((exp_count, 16, 128), F32),
            pltpu.VMEM((exp_count, 16, 128), BF16),
            pltpu.VMEM((3, copies, part, width), BF16),
            dma((2, exp_count)),
            dma((2, exp_count)),
            dma((2, 3, copies)),
            dma((2, exp_count)),
            dma((2, exp_count)),
            dma((2, exp_count)),
            dma((2, exp_count)),
            dma((2, 3, copies)),
        ],
        compiler_params=pltpu.CompilerParams(
            collective_id=0, has_side_effects=True, vmem_limit_bytes=56 * 1024 * 1024
        ),
        cost_estimate=pl.CostEstimate(
            flops=16 * total_rows * hidden * width, bytes_accessed=16 << 20, transcendentals=0
        ),
    )(select, tokens, grad_out, w_gate[0], w_up[0], w_down[0])
    back = [
        lax.dot_general(picks, ret[:, c * cap : (c + 1) * cap].reshape(slots, half), TN, preferred_element_type=F32)
        for c in (0, 1)
    ]
    grad_tokens = jnp.concatenate(back, axis=1).astype(BF16)
    prob_back = ret_prob[:, 0, :cap].reshape(slots, 1).astype(F32)
    grad_probs = jnp.stack(
        [jnp.sum(jnp.where(hit, prob_back, 0.0), axis=0) for hit in hits], axis=1
    ) / probs.astype(F32)
    full = own_grads + jnp.sum(peer_grads.astype(F32), axis=1)
    return (grad_tokens, grad_probs, full[0][None], full[1][None], full[2][None])


def solution(mesh):
    rows = P(("exp", "rep"), None)
    weight = P("exp", "rep", None)
    return jax.shard_map(
        functools.partial(shards, mesh.shape["rep"]),
        mesh=mesh,
        in_specs=(rows, rows, rows, rows, weight, weight, weight),
        out_specs=(rows, rows, weight, weight, weight),
        check_vma=False,
    )
```

time: 198 us -> 128 us (0.65)
  Pallas kernels: 0 us -> 115 us
  waiting for transfers between devices: 101 us -> 0 us
  starting transfers between devices: 37.9 us -> 0 us
  matrix products: 24.1 us -> 0.63 us
  local copies, waits for them, and re-layouts: 22.8 us -> 5.33 us
  other arithmetic: 10.4 us -> 6.04 us
    pallas_call x0 -> x1, Pallas kernels: none -> 115 us  [shards(): pl.pallas_call(functools.partial(layer, exp_count, rep_count, cap), out_s...]
    ppermute x11 -> x0, waiting for transfers between devices: 65.5 us -> none  [swapped(): lax.ppermute(value, axis, [(i, i ^ 1 << stride) for i in range(lax.axis_s...]
    all_to_all x5 -> x0, waiting for transfers between devices: 35.4 us -> none  [the longest x1 18.9 us: shards(): lax.all_to_all(send_tokens, 'exp', split_axis=0, concat_axis=0, tiled=True)]
    all_to_all x5 -> x0, starting transfers between devices: 24.1 us -> none  [the longest x1 6.33 us: shards(): lax.all_to_all(send_probs, 'exp', split_axis=0, concat_axis=0, tiled=True)]
    dot_general x13 -> x2, matrix products: 24.1 us -> 0.63 us  [shards(): lax.dot_general(picks, ret[:, c * cap:(c + 1) * cap].reshape(slots, half)...]
    ppermute x11 -> x0, starting transfers between devices: 13.8 us -> none  [swapped(): lax.ppermute(value, axis, [(i, i ^ 1 << stride) for i in range(lax.axis_s...]
    dynamic_update_slice x12 -> x0, local copies, waits for them, and re-layouts: 11.3 us -> none  [the longest x6 5.7 us: joined_pair(): lax.dynamic_update_slice_in_dim(joined, mine, upper_bit * length, along)]
    add x5 -> x2, other arithmetic: 8.4 us -> 1.98 us  [the longest x1 1.96 us: shards(): full = own_grads + jnp.sum(peer_grads.astype(F32), axis=1)]
  transfers between devices with their start and end apart: 16 -> 0, of which waited for: 11 -> 0; matrix products, arithmetic and copies ran while one was open for 20% -> 0% of each run, Pallas kernels for 0% -> 0%
where the time goes in v1:
time: 128 us; the launch traced here: 127 us
  Pallas kernels  115 us (90%)
  other arithmetic  6.04 us (5%)
  local copies, waits for them, and re-layouts  5.33 us (4%)
    pallas_call x1, Pallas kernels, shards(): pl.pallas_call(functools.partial(layer, exp_count, rep_count, cap), out_s...  115 us

profile of v1, /device:TPU:0, one launch (start us, length us, event | category | flops | bytes accessed | tf_op | source)
XLA Modules:
  0.0 127.4 jit_solution(2857053813928608198)
XLA Ops:
  0.6 0.7 slice_bitcast_fusion.1
  1.4 0.8 copy.16
  2.2 0.1 eq.71
  2.3 0.2 convert_reduce_fusion
  2.5 0.1 reduce_sum.38
  2.7 0.2 slice_reduce_fusion.1
  2.8 0.1 compare_or_fusion
  3.0 0.1 compare_select_fusion.1
  3.1 0.8 fusion.1.select
  3.9 114.7 %shard_map.110 = (bf16[8,80,768]{2,1,0:T(8,128)(2,1)}, bf16[8,16,128]{2,1,0:T(8,128)(2,1)}, f32[3,192,1536]{2,1,0:T(8,128)}, bf16[3,1,192,1536]{3,2,1,0:T(8,128)(2,1)}) custom-call(bf16[8,80,256]{2,1,0:T(8,128)(2,1)} %fusion.1.select, bf16[128,1536]{1,0:T(8,128)(2,1)} %tokens.1, bf16[128,1536]{1,0:T(8,128)(2,1)} %grads.1, bf16[192,1536]{1,0:T(8,128)(2,1)} %bitcast.20, ...), custom_call_target="tpu_custom_call" | custom-call | flops 6039797760 | bytes 16777216 | tf_op jit(solution)/shard_map/pallas_call | solution.py:256
  118.6 0.0 copy-start
  118.6 1.4 %fusion.11 = (bf16[8,40,768]{2,1,0:T(8,128)(2,1)S(1)}, bf16[8,40,768]{2,1,0:T(8,128)(2,1)S(1)}) fusion(bf16[8,80,768]{2,1,0:T(8,128)(2,1)} %get-tuple-element.9), kind=kLoop, calls=%fused_computation.32 | loop fusion | bytes 1966080 | tf_op jit(solution)/shard_map/slice | solution.py:301
  120.0 0.3 convolution_convert_fusion.1
  120.3 0.3 convolution_convert_fusion
  120.6 0.8 pad_maximum_fusion
  121.4 0.7 convert_reduce_fusion.1
  122.1 0.1 reshape.88
  122.2 0.1 select_reduce_fusion.1
  122.3 1.2 maximum_divide_fusion
  123.6 0.0 copy-done
  123.6 2.0 %convert_add_fusion = f32[3,192,1536]{2,1,0:T(8,128)S(1)} fusion(f32[3,192,1536]{2,1,0:T(8,128)S(1)} %copy-done, bf16[3,1,192,1536]{3,2,1,0:T(8,128)(2,1)} %get-tuple-element.12), kind=kLoop, calls=%fused_computation | loop fusion | flops 1769472 | bytes 8847360 | tf_op jit(solution)/shard_map/add | solution.py:309
  125.5 1.9 %fusion.10 = (f32[1,192,1536]{2,1,0:T(8,128)}, f32[1,192,1536]{2,1,0:T(8,128)}, f32[1,192,1536]{2,1,0:T(8,128)}) fusion(f32[3,192,1536]{2,1,0:T(8,128)S(1)} %convert_add_fusion), kind=kLoop, calls=%fused_computation.31 | loop fusion | bytes 7077888 | tf_op jit(solution)/shard_map/slice | solution.py:310
  (3 shorter events, 0.0 us)
Async XLA Ops:
  118.6 5.0 %copy-start = (f32[3,192,1536]{2,1,0:T(8,128)S(1)}, f32[3,192,1536]{2,1,0:T(8,128)}, u32[]{:S(2)}) copy-start(f32[3,192,1536]{2,1,0:T(8,128)} %get-tuple-element.11) | copy-start | bytes 10616836

commit v2 on v1

v2 whole, which is shorter than its diff:
```python
import functools

import jax
import jax.numpy as jnp
from jax import lax
from jax.experimental import pallas as pl
from jax.experimental.pallas import tpu as pltpu
from jax.sharding import PartitionSpec as P

F32 = jnp.float32
BF16 = jnp.bfloat16
NT = (((1,), (1,)), ((), ()))
TN = (((0,), (0,)), ((), ()))


def flipped(index, mask, bits):
    for bit in range(bits):
        if mask >> bit & 1:
            index = index + (1 << bit) - 2 * (1 << bit) * (index // (1 << bit) % 2)
    return index


def dot(a, b, dims=(((1,), (0,)), ((), ()))):
    return lax.dot_general(a, b, dims, preferred_element_type=F32)


def layer(
    exp_count,
    rep_count,
    cap,
    select,
    hits,
    tokens,
    grads,
    w_gate,
    w_up,
    w_down,
    grad_tokens,
    grad_probs,
    own_gate,
    own_up,
    own_down,
    peer_gate,
    peer_up,
    peer_down,
    send,
    recv,
    weights,
    rows,
    row_grads,
    own_units,
    rest_units,
    x_send,
    x_recv,
    keep,
    z_send,
    ret,
    xp_send,
    xp_recv,
    keep_prob,
    zp_send,
    ret_prob,
    grads_out,
    z_sems,
    x_sems,
    y_sems,
    xr_sems,
    zr_sems,
    xp_sems,
    zp_sems,
    g_sems,
):
    exp_bits = exp_count.bit_length() - 1
    rep_bits = rep_count.bit_length() - 1
    copies = rep_count // 2
    exp_at = lax.axis_index("exp")
    rep_at = lax.axis_index("rep")
    count, width = tokens.shape
    half = width // 2
    part = w_gate.shape[0]
    exp_peer = [{"exp": flipped(exp_at, d, exp_bits)} for d in range(exp_count)]
    x_peer = {"rep": flipped(rep_at, 1, rep_bits)}
    y_peer = [{"rep": flipped(rep_at, 2 * f, rep_bits)} for f in range(copies)]
    far = range(exp_count // 4, exp_count // 2)
    near = range(1, exp_count // 4)
    steps = [0, *far, *near]

    barrier = pltpu.get_barrier_semaphore()
    peers = exp_peer[1:] + [x_peer] + y_peer[1:]
    for peer in peers:
        pl.semaphore_signal(barrier, inc=1, device_id=peer, device_id_type=pl.DeviceIdType.MESH)

    def pick(d):
        picked = dot(select[d, :, :count], tokens[...]) + dot(select[d, :, count:], grads[...])
        send[d] = picked.astype(BF16)

    started = []

    def remote(src, dst, sems, at, peer):
        copy = pltpu.make_async_remote_copy(
            src_ref=src,
            dst_ref=dst,
            send_sem=sems.at[(0, *at)],
            recv_sem=sems.at[(1, *at)],
            device_id=peer,
            device_id_type=pl.DeviceIdType.MESH,
        )
        copy.start()
        started.append(copy)
        return copy

    z_in, y_in, x_in = {}, {}, {}
    matrices = (w_gate, w_up, w_down)
    pick(0)
    pick(1)
    pl.semaphore_wait(barrier, len(peers))
    z_in[1] = remote(send.at[1], recv.at[0, 1], z_sems, (1,), exp_peer[1])
    x_in[0] = remote(send.at[0], recv.at[1, 0], x_sems, (0,), x_peer)
    for f in range(1, copies):
        for m in range(3):
            y_in[m, f] = remote(matrices[m], weights.at[m, f], y_sems, (m, f), y_peer[f])
    for step in steps[1:]:
        for d in (2 * step, 2 * step + 1):
            pick(d)
            z_in[d] = remote(send.at[d], recv.at[0, d], z_sems, (d,), exp_peer[d])
    recv[0, 0] = send[0]
    for m in range(3):
        weights[m, 0] = matrices[m][...]

    ones = jnp.ones((16, part * (copies - 1)), BF16)

    def load(step):
        pieces_t, pieces_g = [], []
        for d in (2 * step, 2 * step + 1):
            x_in[d].wait_recv()
            for side in (0, 1):
                block = recv[side, d].astype(F32)
                pieces_t.append(block[:cap])
                pieces_g.append(block[cap:])
        at = pl.ds(step * 4 * cap, 4 * cap)
        rows[at] = jnp.concatenate(pieces_t, axis=0).astype(BF16)
        row_grads[at] = jnp.concatenate(pieces_g, axis=0).astype(BF16)

    def matrix(m, first, last):
        return weights[m, first:last].reshape((last - first) * part, width)

    def forward(step, first, last, units, fresh):
        at = pl.ds(step * 4 * cap, 4 * cap)
        gate = dot(rows[at], matrix(0, first, last), NT)
        up = dot(rows[at], matrix(1, first, last), NT)
        back = dot(row_grads[at], matrix(2, first, last), NT)
        sig = jax.nn.sigmoid(gate)
        act = gate * sig
        hid = act * up
        units[0, at] = (back * up * sig * (1.0 + gate * (1.0 - sig))).astype(BF16)
        units[1, at] = (back * act).astype(BF16)
        units[2, at] = hid.astype(BF16)
        product = hid * back
        wide = (last - first) * part
        pad = jnp.zeros((128 - cap, wide), F32)
        for i in range(4):
            d, side = 2 * step + i // 2, i % 2
            mine = jnp.concatenate([product[i * cap : (i + 1) * cap], pad], axis=0).astype(BF16)
            total = dot(ones[:, :wide], mine, NT)
            if fresh:
                keep_prob[side, d] = total
            else:
                keep_prob[side, d] += total

    def arrive(step):
        for d in (2 * step, 2 * step + 1):
            if d:
                z_in[d].wait_recv()
                x_in[d] = remote(recv.at[0, d], recv.at[1, d], x_sems, (d,), x_peer)

    def early(step):
        load(step)
        forward(step, 0, 1, own_units, True)

    for i, step in enumerate(steps):
        arrive(step)
        if i:
            early(steps[i - 1])
    for copy in y_in.values():
        copy.wait_recv()
    for step in steps[:-1]:
        forward(step, 1, copies, rest_units, False)
    load(steps[-1])
    forward(steps[-1], 1, copies, rest_units, True)

    g_in = []
    rights = (rows, rows, row_grads)
    own_grads = (own_gate, own_up, own_down)
    peer_grads = (peer_gate, peer_up, peer_down)
    for m in range(3):
        for f in range(1, copies):
            product = dot(rest_units[m, :, (f - 1) * part : f * part], rights[m][...], TN)
            grads_out[m, f] = product.astype(BF16)
            g_in.append(remote(grads_out.at[m, f], peer_grads[m].at[f - 1], g_sems, (m, f), y_peer[f]))
    forward(steps[-1], 0, 1, own_units, False)

    xr_in, xp_in = {}, {}

    def backward(step):
        at = pl.ds(step * 4 * cap, 4 * cap)
        partial = jnp.zeros((4 * cap, width), F32)
        for m in (0, 1):
            partial += dot(own_units[m, at], matrix(m, 0, 1))
            partial += dot(rest_units[m, at], matrix(m, 1, copies))
        for i in range(4):
            d, side = 2 * step + i // 2, i % 2
            piece = partial[i * cap : (i + 1) * cap]
            folded = jnp.concatenate([piece[:, :half], piece[:, half:]], axis=0)
            if side:
                x_send[d] = folded.astype(BF16)
                xp_send[d] = keep_prob[1, d].astype(BF16)
                xr_in[d] = remote(x_send.at[d], x_recv.at[d], xr_sems, (d,), x_peer)
                xp_in[d] = remote(xp_send.at[d], xp_recv.at[d], xp_sems, (d,), x_peer)
            else:
                keep[d] = folded

    zr_in = []

    def give_back(d):
        xp_in[d].wait_recv()
        xr_in[d].wait_recv()
        total = (keep[d] + x_recv[d].astype(F32)).astype(BF16)
        total_prob = (keep_prob[0, d] + xp_recv[d].astype(F32)).astype(BF16)
        if d == 0:
            ret[0] = total
            ret_prob[0] = total_prob
        else:
            z_send[d] = total
            zp_send[d] = total_prob
            zr_in.append(remote(z_send.at[d], ret.at[d], zr_sems, (d,), exp_peer[d]))
            zr_in.append(remote(zp_send.at[d], ret_prob.at[d], zp_sems, (d,), exp_peer[d]))

    back_steps = [*far, *near, 0]
    for step in back_steps:
        backward(step)
    for m, own in enumerate(own_grads):
        own[...] = dot(own_units[m], rights[m][...], TN)
        if m < 2:
            give_back(2 * back_steps[m])
            give_back(2 * back_steps[m] + 1)
    for step in back_steps[2:]:
        give_back(2 * step)
        give_back(2 * step + 1)
    for copy in zr_in:
        copy.wait_recv()
    picks = jnp.where(select[...].astype(F32) != 0.0, 1.0, 0.0).astype(BF16)
    blocks = exp_count * 2 * cap
    total = dot(picks.reshape(blocks, 2 * count), ret[...].reshape(blocks, half), TN)
    grad_tokens[:, :half] = total[:count].astype(BF16)
    grad_tokens[:, half:] = total[count:].astype(BF16)
    for k in (0, 1):
        probs_k = jnp.zeros((16, count), F32)
        for d in range(exp_count):
            probs_k += dot(ret_prob[d, :, :cap], hits[k, d])
        grad_probs[k] = probs_k
    for copy in g_in:
        copy.wait_recv()
    for copy in started:
        copy.wait_send()


def shards(rep_count, tokens, grad_out, expert_ids, probs, w_gate, w_up, w_down):
    count, width = tokens.shape
    exp_count = lax.axis_size("exp")
    copies = rep_count // 2
    part = w_gate.shape[1]
    hidden = copies * part
    cap = -(-(5 * count // (2 * exp_count)) // 8) * 8
    slots = exp_count * cap
    half = width // 2
    columns = expert_ids.T
    chosen = columns.reshape(-1)
    pair = jnp.arange(2 * count, dtype=jnp.int32)
    same = (chosen[:, None] == chosen[None, :]) & (pair[:, None] < pair[None, :])
    ranks = jnp.sum(same.astype(jnp.int32), axis=0)
    slot_pair = ((chosen ^ lax.axis_index("exp")) * cap + ranks).reshape(2, count)
    slot = jnp.arange(slots, dtype=jnp.int32)[:, None]
    found = [slot_pair[k][None, :] == slot for k in (0, 1)]
    hits = jnp.stack(found).astype(BF16).reshape(2, exp_count, cap, count)
    prob_pair = probs.T
    picks = (found[0] | found[1]).astype(BF16)
    scaled = jnp.where(found[0], prob_pair[0][None, :], jnp.where(found[1], prob_pair[1][None, :], 0))
    zero = jnp.zeros((exp_count, cap, count), BF16)
    select = jnp.concatenate(
        [
            jnp.concatenate([picks.reshape(exp_count, cap, count), zero], axis=2),
            jnp.concatenate([zero, scaled.astype(BF16).reshape(exp_count, cap, count)], axis=2),
        ],
        axis=1,
    )
    vmem = pl.BlockSpec(memory_space=pltpu.VMEM)
    total_rows = 2 * slots
    blocks = (exp_count, 2 * cap, half)
    prob_blocks = (exp_count, 16, 128)
    dma = pltpu.SemaphoreType.DMA
    grad_tokens, pair_probs, *parts = pl.pallas_call(
        functools.partial(layer, exp_count, rep_count, cap),
        out_shape=(
            jax.ShapeDtypeStruct((count, width), BF16),
            jax.ShapeDtypeStruct((2, 16, count), F32),
            *[jax.ShapeDtypeStruct((part, width), F32)] * 3,
            *[jax.ShapeDtypeStruct((copies - 1, part, width), BF16)] * 3,
        ),
        in_specs=[vmem] * 7,
        out_specs=(vmem,) * 8,
        scratch_shapes=[
            pltpu.VMEM((exp_count, 2 * cap, width), BF16),
            pltpu.VMEM((2, exp_count, 2 * cap, width), BF16),
            pltpu.VMEM((3, copies, part, width), BF16),
            pltpu.VMEM((total_rows, width), BF16),
            pltpu.VMEM((total_rows, width), BF16),
            pltpu.VMEM((3, total_rows, part), BF16),
            pltpu.VMEM((3, total_rows, hidden - part), BF16),
            pltpu.VMEM(blocks, BF16),
            pltpu.VMEM(blocks, BF16),
            pltpu.VMEM(blocks, F32),
            pltpu.VMEM(blocks, BF16),
            pltpu.VMEM(blocks, BF16),
            pltpu.VMEM(prob_blocks, BF16),
            pltpu.VMEM(prob_blocks, BF16),
            pltpu.VMEM((2, *prob_blocks), F32),
            pltpu.VMEM(prob_blocks, BF16),
            pltpu.VMEM(prob_blocks, BF16),
            pltpu.VMEM((3, copies, part, width), BF16),
            dma((2, exp_count)),
            dma((2, exp_count)),
            dma((2, 3, copies)),
            dma((2, exp_count)),
            dma((2, exp_count)),
            dma((2, exp_count)),
            dma((2, exp_count)),
            dma((2, 3, copies)),
        ],
        compiler_params=pltpu.CompilerParams(
            collective_id=0, has_side_effects=True, vmem_limit_bytes=56 * 1024 * 1024
        ),
        cost_estimate=pl.CostEstimate(
            flops=16 * total_rows * hidden * width, bytes_accessed=16 << 20, transcendentals=0
        ),
    )(select, hits, tokens, grad_out, w_gate[0], w_up[0], w_down[0])
    grad_probs = (pair_probs[:, 0, :] / prob_pair.astype(F32)).T
    full = [
        (own + jnp.sum(peer.astype(F32), axis=0))[None] for own, peer in zip(parts[:3], parts[3:])
    ]
    return (grad_tokens, grad_probs, *full)


def solution(mesh):
    rows = P(("exp", "rep"), None)
    weight = P("exp", "rep", None)
    return jax.shard_map(
        functools.partial(shards, mesh.shape["rep"]),
        mesh=mesh,
        in_specs=(rows, rows, rows, rows, weight, weight, weight),
        out_specs=(rows, rows, weight, weight, weight),
        check_vma=False,
    )
```

time: 128 us -> 127 us (level)
  other arithmetic: 6.04 us -> 9.5 us
  local copies, waits for them, and re-layouts: 5.33 us -> 2.21 us
    broadcast_in_dim x0 -> x2, other arithmetic: none -> 5.56 us  [shards(): (own + jnp.sum(peer.astype(F32), axis=0))[None]]
    slice x3 -> x2, local copies, waits for them, and re-layouts: 3.44 us -> 0.71 us  [the longest x1 0.7 us: shards(): grad_probs = (pair_probs[:, 0, :] / prob_pair.astype(F32)).T]
    add x2 -> x1, other arithmetic: 1.98 us -> 0.69 us  [shards(): (chosen ^ lax.axis_index('exp')) * cap + ranks]
where the time goes in v2:
time: 127 us; the launch traced here: 126 us
  Pallas kernels  114 us (90%)
  other arithmetic  9.5 us (7%)
  local copies, waits for them, and re-layouts  2.21 us (2%)
    pallas_call x1, Pallas kernels, shards(): pl.pallas_call(functools.partial(layer, exp_count, rep_count, cap), out_s...  114 us
    broadcast_in_dim x2, other arithmetic, shards(): (own + jnp.sum(peer.astype(F32), axis=0))[None]  5.56 us

profile of v2, /device:TPU:0, one launch (start us, length us, event | category | flops | bytes accessed | tf_op | source)
XLA Modules:
  0.0 126.3 jit_solution(11863745731021414999)
XLA Ops:
  0.6 0.9 convert_reduce_fusion
  1.5 0.7 multiply_add_fusion.1
  2.2 0.7 slice_bitcast_fusion.1
  2.9 0.1 compare_or_fusion
  3.1 0.1 compare_select_fusion.1
  3.2 0.1 broadcast_compare_fusion.1
  3.3 0.7 add_convert_fusion.hits
  4.0 0.8 fusion.4.select
  4.8 0.0 copy-start.4
  4.8 113.9 %shard_map.110 = (bf16[128,1536]{1,0:T(8,128)(2,1)}, f32[2,16,128]{2,1,0:T(8,128)}, f32[192,1536]{1,0:T(8,128)}, f32[192,1536]{1,0:T(8,128)}, f32[192,1536]{1,0:...) custom-call(bf16[8,80,256]{2,1,0:T(8,128)(2,1)} %fusion.4.select, ...), custom_call_target="tpu_custom_call" | custom-call | flops 6039797760 | bytes 16777216 | tf_op jit(solution)/shard_map/pallas_call | solution.py:301
  118.7 0.7 slice.21
  119.4 0.0 copy-done.4
  119.4 0.6 fusion.6
  119.9 0.0 copy-start
  119.9 0.0 copy-start.1
  119.9 0.0 copy-start.2
  119.9 2.7 %fusion.2 = f32[1,192,1536]{2,1,0:T(8,128)} fusion(f32[192,1536]{1,0:T(8,128)} %get-tuple-element.15, bf16[1,192,1536]{2,1,0:T(8,128)(2,1)} %get-tuple-element.16), kind=kLoop, calls=%fused_computation.5 | loop fusion | flops 589824 | bytes 2949120 | tf_op jit(solution)/shard_map/broadcast_in_dim | solution.py:348
  122.7 0.0 copy-done
  122.7 0.0 copy-done.1
  122.7 0.0 copy-done.2
  122.7 0.0 copy-start.3
  122.7 2.8 %fusion = (f32[1,192,1536]{2,1,0:T(8,128)}, f32[1,192,1536]{2,1,0:T(8,128)}) fusion(f32[192,1536]{1,0:T(8,128)S(1)} %copy-done.1, bf16[1,192,1536]{2,1,0:T(8,128)(2,1)} %get-tuple-element.20, f32[192,1536]{1,0:T(8,128)S(1)} %copy-done, bf16[1,192,1536]{2,1,0:T(8,128)(2,1)S(1)} %copy-done.2), kind=kLoop, calls=%fused_computation.1 | loop fusion | flops 1179648 | bytes 5898240 | tf_op jit(solution)/shard_map/broadcast_in_dim | solution.py:348
  125.5 0.0 copy-done.3
  125.5 0.7 copy.13
  (3 shorter events, 0.0 us)
Async XLA Ops:
  4.8 114.6 %copy-start.4 = (bf16[128,2]{0,1:T(2,128)(2,1)S(1)}, bf16[128,2]{0,1:T(2,128)(2,1)}, u32[]{:S(2)}) copy-start(bf16[128,2]{0,1:T(2,128)(2,1)} %param.10) | copy-start | bytes 1540
  119.9 2.7 %copy-start = (f32[192,1536]{1,0:T(8,128)S(1)}, f32[192,1536]{1,0:T(8,128)}, u32[]{:S(2)}) copy-start(f32[192,1536]{1,0:T(8,128)} %get-tuple-element.17) | copy-start | bytes 3538948
  119.9 2.7 %copy-start.1 = (f32[192,1536]{1,0:T(8,128)S(1)}, f32[192,1536]{1,0:T(8,128)}, u32[]{:S(2)}) copy-start(f32[192,1536]{1,0:T(8,128)} %get-tuple-element.19) | copy-start | bytes 3538948
  119.9 2.7 %copy-start.2 = (bf16[1,192,1536]{2,1,0:T(8,128)(2,1)S(1)}, bf16[1,192,1536]{2,1,0:T(8,128)(2,1)}, u32[]{:S(2)}) copy-start(bf16[1,192,1536]{2,1,0:T(8,128)(2,1)} %get-tuple-element.18) | copy-start | bytes 1769476
  122.7 2.9 %copy-start.3 = (bf16[128,1536]{1,0:T(8,128)(2,1)S(1)}, bf16[128,1536]{1,0:T(8,128)(2,1)}, u32[]{:S(2)}) copy-start(bf16[128,1536]{1,0:T(8,128)(2,1)} %get-tuple-element.34) | copy-start | bytes 1179652
